TPU v7x, 256 devices: a whole 4x4x8 slice. The times are simulated.
256 devices in a mesh: section: 8 (over y_hi, x), seq: 32 (over z, y_lo, core).
Axes of the slice: x: 4, y: 4 (y_hi: 2, y_lo: 2; y = y_hi * 2 + y_lo), z: 8, core: 2. Of those that a mesh axis runs over, the one named last changes fastest.
Arguments:
- text_embed: bfloat16 [98304, 8192], P('seq', 'section')
- vis_rows: bfloat16 [90112, 8192], P('seq', 'section')
- norm_gain: bfloat16 [8192], P('section'), may hold values from 0.25 to 1.75
- w_kv: bfloat16 [8192, 1024], P('section', 'seq'), may hold values from -0.125 to 0.125
- block_counts: int32 [32], replicated, may hold values from 1 to 12, 352 in all
- block_offset: int32 [32], replicated, may hold values from 0 to 11
Outputs:
- key_value: bfloat16 [1024, 98304], P('section', 'seq')
Inputs may be any that keep to these rules, and one draw needn't show every extreme that they name: `block_counts`: they sum to 352, and the largest is exactly 12.
All inputs are finite; a program needn't handle non-finite values.
Results may differ from a plain program's by a relative error of at most 0.015.
Values may be sent and summed in bfloat16 or wider, within the bound.
A program may use at most 128 MiB of HBM per device.

v0:
```python
import jax
import jax.numpy as jnp
from jax import lax
from jax.sharding import PartitionSpec as P

D = 8192
TILE_ROWS = 256


epsilon = 1e-06


def row_squares_of(rows):
    rows_f32 = rows.astype(jnp.float32)
    return jnp.sum(rows_f32 * rows_f32, axis=1)


def normalize(rows, squares, gain_f32):
    return (rows.astype(jnp.float32) * lax.rsqrt(squares / D + epsilon)[:, None] * gain_f32).astype(
        jnp.bfloat16
    )


def make_term(normed, w_full):
    return lax.dot_general(
        w_full, normed, (((0,), (1,)), ((), ())), preferred_element_type=jnp.float32
    )


def project(normed, w_full):
    return lax.psum_scatter(
        make_term(normed, w_full).astype(jnp.bfloat16), "section", scatter_dimension=0, tiled=True
    ).astype(jnp.float32)


def local(text_embed, vis_rows, norm_gain, w_kv, block_counts, block_offset):
    shard_count = lax.axis_size("seq")
    shard_id = lax.axis_index("seq")
    rows_dev, feat_dev = text_embed.shape
    blocks_dev = rows_dev // TILE_ROWS
    tiles_dev = vis_rows.shape[0] // TILE_ROWS
    w_full = lax.all_gather(w_kv, "seq", axis=1, tiled=True)
    run_ends = jnp.cumsum(block_counts)
    run_starts = run_ends - block_counts
    slot_ids = shard_id + shard_count * jnp.arange(tiles_dev, dtype=jnp.int32)
    owners = jnp.sum((run_ends[None, :] <= slot_ids[:, None]).astype(jnp.int32), axis=1)
    peer_ids = jnp.arange(shard_count, dtype=jnp.int32)
    send_select = (peer_ids[:, None] == owners[None, :]).astype(jnp.bfloat16)
    order_in = (peer_ids - run_starts[shard_id]) % shard_count
    present = order_in < block_counts[shard_id]
    slot_block = (order_in + block_offset[shard_id]) % blocks_dev
    block_ids = jnp.arange(blocks_dev, dtype=jnp.int32)
    place_select = ((block_ids[:, None] == slot_block[None, :]) & present[None, :]).astype(
        jnp.bfloat16
    )
    vision_rows = jnp.repeat(jnp.sum(place_select.astype(jnp.float32), axis=1) > 0.5, TILE_ROWS)
    gain_f32 = norm_gain.astype(jnp.float32)
    tile_flat = vis_rows.reshape(tiles_dev, TILE_ROWS * feat_dev)
    outgoing = jnp.dot(send_select, tile_flat, preferred_element_type=jnp.float32).astype(
        jnp.bfloat16
    )
    outgoing = outgoing.reshape(shard_count, TILE_ROWS, feat_dev)
    incoming = lax.all_to_all(outgoing, "seq", split_axis=0, concat_axis=0, tiled=True)
    placed = (
        jnp.dot(
            place_select,
            incoming.reshape(shard_count, TILE_ROWS * feat_dev),
            preferred_element_type=jnp.float32,
        )
        .astype(jnp.bfloat16)
        .reshape(rows_dev, feat_dev)
    )
    merged = jnp.where(vision_rows[:, None], placed, text_embed)
    squares = lax.psum(row_squares_of(merged), "section")
    normed = normalize(merged, squares, gain_f32)
    result = project(normed, w_full).astype(jnp.bfloat16)
    return result


def solution(mesh):
    return jax.shard_map(
        local,
        mesh=mesh,
        in_specs=(
            P("seq", "section"),
            P("seq", "section"),
            P("section"),
            P("section", "seq"),
            P(),
            P(),
        ),
        out_specs=P("section", "seq"),
        check_vma=False,
    )
```

profile of v0, /device:TPU:1, one launch (start us, length us, event | category | flops | bytes accessed | tf_op | source)
XLA Modules:
  0.0 649.6 jit_solution(10353351066310960291)
XLA Ops:
  6.5 0.7 copy.13
  7.3 0.1 reduce-window.8
  7.3 0.1 reduce
  7.4 8.0 %reshape.71 = bf16[11,262144]{1,0:T(8,128)(2,1)} reshape(bf16[2816,1024]{1,0:T(8,128)(2,1)} %param.7) | data formatting | bytes 11534336 | tf_op jit(solution)/shard_map/reshape | solution.py:58
  15.4 0.2 convert_reduce_fusion
  15.6 11.4 %convolution_convert_fusion = bf16[32,262144]{1,0:T(8,128)(2,1)} fusion(bf16[11,262144]{1,0:T(8,128)(2,1)} %reshape.71, s32[11]{0:T(128)S(1)} %convert_reduce_fusion), kind=kOutput, calls=%fused_computation | convolution fusion | flops 192938336 | bytes 22544428 | tf_op jit(solution)/shard_map/dot_general | solution.py:59
  27.0 18.7 %copy.17 = bf16[4,8,256,1024]{3,2,1,0:T(8,128)(2,1)} copy(bf16[4,8,256,1024]{3,1,2,0:T(8,128)(2,1)} %bitcast.14) | data formatting | bytes 33554432
  45.7 0.0 copy-start.1
  45.7 0.0 copy-start.2
  45.7 0.0 copy-start
  45.7 11.3 %all-to-all-start = ((bf16[32,256,1024]{2,1,0:T(8,128)(2,1)}), bf16[32,256,1024]{2,1,0:T(8,128)(2,1)}, u32[]{:S(2)}, u32[]{:S(2)}) async-start(bf16[32,256,1024]{2,1,0:T(8,128)(2,1)} %bitcast.16), calls=%async_computation | async-start | bytes 33554432 | tf_op jit(solution)/shard_map/all_to_all | solution.py:63
  57.0 0.0 all-gather.2.cloned.1.call-start
  57.1 0.7 all-gather.2.cloned.1.call-update
  57.8 0.2 reduce-scatter.4.cloned.1.call-start
  58.0 0.0 copy-done.1
  58.0 0.7 dynamic_slice.11
  58.7 0.6 dynamic_slice.9
  59.3 0.0 copy-done.2
  59.3 0.6 dynamic_slice.10
  59.9 1.2 and_select_fusion
  61.1 1.3 broadcast_compare_fusion.1
  62.4 0.1 convert_reduce_fusion.1
  62.5 0.1 broadcast_in_dim.9
  62.6 0.0 copy-done
  62.6 359.9 %all-to-all-done = bf16[32,256,1024]{2,1,0:T(8,128)(2,1)} async-done(((bf16[32,256,1024]{2,1,0:T(8,128)(2,1)}), bf16[32,256,1024]{2,1,0:T(8,128)(2,1)}, u32[]{:S(2)}, u32[]{:S(2)}) %all-to-all-start) | async-done | bytes 16777248 | tf_op jit(solution)/shard_map/all_to_all | solution.py:63
  422.6 18.7 %copy.18 = bf16[4,8,256,1024]{3,1,2,0:T(8,128)(2,1)} copy(bf16[4,8,256,1024]{3,2,1,0:T(8,128)(2,1)} %bitcast.8) | data formatting | bytes 33554432
  441.2 11.3 %convolution_convert_fusion.1 = bf16[12,262144]{1,0:T(8,128)(2,1)} fusion(bf16[32,262144]{1,0:T(8,128)(2,1)} %bitcast.15, s32[32]{0:T(128)S(1)} %and_select_fusion, pred[32]{0:T(512)(128)(4,1)S(1)} %broadcast_compare_fusion.1), kind=kOutput, calls=%fused_computation.1 | convolution fusion | flops 204473088 | bytes 23068832 | tf_op jit(solution)/shard_map/dot_general | solution.py:65
  452.6 8.6 %reshape.74 = bf16[3072,1024]{1,0:T(8,128)(2,1)} reshape(bf16[12,262144]{1,0:T(8,128)(2,1)} %convolution_convert_fusion.1) | data formatting | bytes 12582912 | tf_op jit(solution)/shard_map/reshape | solution.py:71
  461.1 6.3 fusion
  467.5 34.4 %psum.7 = f32[3072]{0:T(1024)S(1)} all-reduce(f32[3072]{0:T(1024)S(1)} %fusion), channel_id=1, replica_groups=mesh['section'=8,'seq'=32] {'section'}, use_global_device_ids=true, to_apply=%region_4.5 | all-reduce | flops 3072 | bytes 24576 | tf_op jit(solution)/shard_map/psum | solution.py:74
  501.9 0.0 all-gather.2.cloned.1.call-done
  501.9 13.2 %convert_bitcast_fusion = bf16[1024,3072]{0,1:T(8,128)(2,1)} fusion(bf16[1024,1024]{0,1:T(8,128)(2,1)} %all-gather.2.cloned.1.call-done, f32[1024]{0:T(1024)S(1)} %convert_element_type.40, f32[3072]{0:T(1024)S(1)} %add_rsqrt_fusion, bf16[3072,1024]{1,0:T(8,128)(2,1)} %reshape.74, bf16[3072,1024]{1,0:T(8,128)(2,1)} %param.6, ...), kind=kOutput, calls=%fused_computation.8 | convolution fusion | flops 6461325312 | bytes 20990976 | tf_op jit(solution)/shard_map/dot_general | solution.py:25
  515.1 8.6 %copy.15 = bf16[1024,3072]{1,0:T(8,128)(2,1)} copy(bf16[1024,3072]{0,1:T(8,128)(2,1)} %convert_bitcast_fusion) | data formatting | bytes 12582912
  523.7 0.0 reduce-scatter.4.cloned.1.call-update
  523.8 119.0 %reduce-scatter.4.cloned.1.call-done = bf16[128,3072]{1,0:T(8,128)(2,1)} async-done(((bf16[1024,3072]{1,0:T(8,128)(2,1)}), bf16[128,3072]{1,0:T(8,128)(2,1)}) %reduce-scatter.4.cloned.1.call-update) | async-done | bytes 786448 | tf_op jit(solution)/shard_map/reduce_scatter | solution.py:31
  (6 shorter events, 0.0 us)
Async XLA Ops:
  45.7 12.3 %copy-start.1 = (s32[32]{0:T(128)S(1)}, s32[32]{0:T(128)}, u32[]{:S(2)}) copy-start(s32[32]{0:T(128)} %param.10) | copy-start | bytes 388
  45.7 13.6 %copy-start.2 = (s32[32]{0:T(128)S(1)}, s32[32]{0:T(128)}, u32[]{:S(2)}) copy-start(s32[32]{0:T(128)} %param.11) | copy-start | bytes 388
  45.7 16.9 %copy-start = (bf16[1024]{0:T(1024)(128)(2,1)S(1)}, bf16[1024]{0:T(1024)(128)(2,1)}, u32[]{:S(2)}) copy-start(bf16[1024]{0:T(1024)(128)(2,1)} %param.8) | copy-start | bytes 6148
  45.7 376.9 %all-to-all-start = ((bf16[32,256,1024]{2,1,0:T(8,128)(2,1)}), bf16[32,256,1024]{2,1,0:T(8,128)(2,1)}, u32[]{:S(2)}, u32[]{:S(2)}) async-start(bf16[32,256,1024]{2,1,0:T(8,128)(2,1)} %bitcast.16), calls=%async_computation | async-start | bytes 33554432 | tf_op jit(solution)/shard_map/all_to_all | solution.py:63
  57.0 444.8 %all-gather.2.cloned.1.call-start = ((), (), s32[]{:S(2)}) async-start(), calls=%async_computation.2 | async-start | bytes 2162688 | tf_op jit(solution)/shard_map/all_gather | solution.py:42
  57.8 585.0 %reduce-scatter.4.cloned.1.call-start = ((), (), s32[]{:S(2)}) async-start(), calls=%async_computation.3 | async-start | bytes 7077888 | tf_op jit(solution)/shard_map/reduce_scatter | solution.py:31
Sparse Core Ops, SparseCore 0:
  59.7 99.4 all-gather.1
  523.9 118.8 reduce-scatter.3
where the time goes:
time: 651 us; the launch traced here: 650 us
  waiting for transfers between devices  480 us (74%)
  local copies, waits for them, and re-layouts  65.2 us (10%)
  matrix products  36 us (6%)
  blocking collectives  34.4 us (5%)
  between operations  13.5 us (2%)
  starting transfers between devices  11.6 us (2%)
  other arithmetic  9.36 us (1%)
    all_to_all x1, waiting for transfers between devices, local(): lax.all_to_all(outgoing, 'seq', split_axis=0, concat_axis=0, tiled=True)  360 us
    reduce_scatter x1, waiting for transfers between devices, project(): lax.psum_scatter(make_term(normed, w_full).astype(jnp.bfloat16), 'section...  119 us
    unnamed x9, local copies, waits for them, and re-layouts  46 us
    psum x1, blocking collectives, local(): squares = lax.psum(row_squares_of(merged), 'section')  34.4 us
    dot_general x1, matrix products, make_term(): lax.dot_general(w_full, normed, (((0,), (1,)), ((), ())), preferred_eleme...  13.2 us
  transfers between devices with their start and end apart: 3, of which 2 were waited for; matrix products, arithmetic and copies ran while one was open for 8% of the time, Pallas kernels for 0%

commit v1 on v0

v1 whole, which is shorter than its diff:
```python
import functools

import jax
import jax.numpy as jnp
from jax import lax
from jax.experimental import pallas as pl
from jax.experimental.pallas import tpu as pltpu
from jax.sharding import PartitionSpec as P

D = 8192
TILE_ROWS = 256
SLOTS = 352
TILES = 11
BLOCKS = 12
FEAT = 1024
KEYS = 128
MESH = pl.DeviceIdType.MESH
epsilon = 1e-06


def kernel(
    rounds,
    counts,
    offsets,
    text_hbm,
    vis_hbm,
    gain_ref,
    wt_ref,
    out_ref,
    starts,
    x_buf,
    text_buf,
    give_buf,
    got_buf,
    w_buf,
    part,
    near_in,
    last_in,
    near_sum,
    pair_out,
    own_sum,
    pair_in,
    done,
    sq_own,
    sq_all,
    row_scale,
    route_out,
    route_in,
    quad_out,
    final,
    local_sem,
    w_quad_sem,
    w_ring_sem,
    w_mate_sem,
    w_send_sem,
    give_sem,
    sq_sem,
    near_sem,
    last_sem,
    pair_sem,
    step_send_sem,
    route_sem,
    quad_sem,
    text_sem,
):
    total = TILES + rounds
    group = lax.axis_index("section")
    shard = lax.axis_index("seq")
    x_pos, y_hi = lax.rem(group, 4), lax.div(group, 4)
    z_pos, rank = lax.div(shard, 4), lax.rem(shard, 4)
    core = lax.rem(shard, 2)
    half = core
    x_up = y_hi * 4 + lax.rem(x_pos + 1, 4)
    x_down = y_hi * 4 + lax.rem(x_pos + 3, 4)
    y_pair = (1 - y_hi) * 4 + x_pos
    core_mate = z_pos * 4 + rank + 1 - 2 * core

    def quad_mate(step):
        return z_pos * 4 + lax.rem(rank + step, 4)

    def z_mate(step):
        return lax.rem(z_pos + step, 8) * 4 + rank

    def z_at(step):
        return lax.rem(z_pos + step + 8, 8)

    def send(src, dst, send_sem, recv_sem, to_group, to_shard):
        pltpu.make_async_remote_copy(
            src_ref=src,
            dst_ref=dst,
            send_sem=send_sem,
            recv_sem=recv_sem,
            device_id=(to_group, to_shard),
            device_id_type=MESH,
        ).start()

    def wait(ref, sem):
        pltpu.make_async_copy(ref, ref, sem).wait()

    text_copy = pltpu.make_async_copy(text_hbm, text_buf, local_sem.at[0])
    vis_copy = pltpu.make_async_copy(vis_hbm, x_buf.at[pl.ds(0, TILES)], local_sem.at[1])
    text_copy.start()
    vis_copy.start()

    barrier = pltpu.get_barrier_semaphore()

    def greet(to_group, to_shard):
        pl.semaphore_signal(barrier, inc=1, device_id=(to_group, to_shard), device_id_type=MESH)

    for step in range(1, 8):
        greet(lax.rem(group + step, 8), shard)
        greet(group, z_mate(step))
    for step in range(1, 4):
        greet(group, quad_mate(step))

    sq_own[...] = jnp.zeros_like(sq_own)
    w_buf[shard] = (wt_ref[...].astype(jnp.float32) * gain_ref[...].astype(jnp.float32)).astype(jnp.bfloat16)

    def scan(idx, running):
        starts[idx] = running
        return running + counts[idx]

    starts[32] = lax.fori_loop(0, 32, scan, jnp.int32(0))
    my_count, my_offset, my_start = counts[shard], offsets[shard], starts[shard]
    spare_0 = BLOCKS - counts[shard - core]
    spare_1 = BLOCKS - counts[shard - core + 1]
    spare = spare_0 + spare_1
    cut = lax.shift_right_logical(spare + 1, 1)

    pl.semaphore_wait(barrier, 17)

    for step in range(1, 4):
        send(w_buf.at[shard], w_buf.at[shard], w_send_sem, w_quad_sem, group, quad_mate(step))

    text_copy.wait()

    def give(idx, carry):
        number = idx + jnp.where(core == 0, cut, 0)
        give_buf[idx] = text_buf[lax.rem(my_offset + my_count + number, BLOCKS)]
        return carry

    lax.fori_loop(0, rounds, give, 0)
    send(give_buf, got_buf, give_sem.at[0], give_sem.at[1], group, core_mate)

    wait(w_buf.at[pl.ds(0, 3)], w_quad_sem)

    def w_half(quad):
        return w_buf.at[pl.ds(quad * 4 + half * 2, 2)]

    def w_mate_send(quad):
        send(w_half(quad), w_half(quad), w_send_sem, w_mate_sem, group, core_mate)

    def ring_step(step):
        up, down = z_at(1 - step), z_at(step - 1)
        if step < 4:
            send(w_half(up), w_half(up), w_send_sem, w_ring_sem.at[0, step - 1], group, z_mate(1))
            send(w_half(down), w_half(down), w_send_sem, w_ring_sem.at[1, step - 1], group, z_mate(7))
        else:
            up_piece = w_buf.at[up * 4 + half * 2]
            down_piece = w_buf.at[down * 4 + half * 2 + 1]
            send(up_piece, up_piece, w_send_sem, w_ring_sem.at[0, 3], group, z_mate(1))
            send(down_piece, down_piece, w_send_sem, w_ring_sem.at[1, 3], group, z_mate(7))

    def ring_wait(step):
        pieces = 2 if step < 4 else 1
        wait(w_buf.at[pl.ds(0, pieces)], w_ring_sem.at[0, step - 1])
        wait(w_buf.at[pl.ds(0, pieces)], w_ring_sem.at[1, step - 1])

    def squares(idx, carry):
        rows = x_buf[idx].astype(jnp.float32)
        rows = rows * rows
        lanes = rows[:, :128]
        for part_idx in range(1, FEAT // 128):
            lanes = lanes + rows[:, part_idx * 128 : (part_idx + 1) * 128]
        sq_own[pl.ds(idx, 1), :] = jnp.sum(lanes.T, axis=0, keepdims=True)
        return carry

    ring_step(1)
    vis_copy.wait()
    lax.fori_loop(0, 4, squares, 0)
    ring_wait(1)
    ring_step(2)
    w_mate_send(z_at(-1))
    w_mate_send(z_at(1))
    lax.fori_loop(4, 8, squares, 0)
    ring_wait(2)
    ring_step(3)
    w_mate_send(z_at(-2))
    w_mate_send(z_at(2))
    lax.fori_loop(8, TILES, squares, 0)
    ring_wait(3)
    ring_step(4)
    w_mate_send(z_at(-3))
    w_mate_send(z_at(3))

    wait(got_buf, give_sem.at[1])

    def pick(idx, carry):
        number = jnp.maximum(jnp.minimum(idx + core * cut, spare - 1), 0)
        of_first = number < spare_0
        mine = of_first == (core == 0)
        order = jnp.where(of_first, number, number - spare_0)
        here = lax.rem(my_offset + my_count + order, BLOCKS)
        there = jnp.where(core == 0, number - spare_0, number - cut)
        there = jnp.maximum(jnp.minimum(there, rounds - 1), 0)
        x_buf[TILES + idx] = lax.select(mine, text_buf[here], got_buf[there])
        return carry

    lax.fori_loop(0, rounds, pick, 0)
    lax.fori_loop(TILES, total, squares, 0)
    for step in range(1, 8):
        send(sq_own, sq_all.at[group], sq_sem.at[0], sq_sem.at[1], lax.rem(group + step, 8), shard)
    sq_all[group] = sq_own[...]

    ring_wait(4)
    w_mate_send(z_at(4))
    wait(w_buf.at[pl.ds(0, 14)], w_mate_sem)

    far = lax.rem(x_pos + 2, 4)
    up_x = lax.rem(x_pos + 1, 4)
    down_x = lax.rem(x_pos + 3, 4)

    def step_body(step, carry):
        @pl.when(step < total)
        def _():
            rows = x_buf[step]
            res = lax.dot_general(
                w_buf[...].reshape(1024, FEAT),
                rows,
                (((1,), (1,)), ((), ())),
                preferred_element_type=jnp.float32,
            )
            part[step] = res.astype(jnp.bfloat16).reshape(8, KEYS, TILE_ROWS)
            send(part.at[step, 4 + far], near_in.at[step, 0], step_send_sem.at[0], near_sem.at[step], x_up, shard)
            send(part.at[step, far], near_in.at[step, 1], step_send_sem.at[0], near_sem.at[step], x_down, shard)

        @pl.when((step >= 1) & (step <= total))
        def _():
            at = step - 1
            wait(near_in.at[at], near_sem.at[at])
            near_sum[at, 0] = (
                near_in[at, 0].astype(jnp.float32) + part[at, 4 + up_x].astype(jnp.float32)
            ).astype(jnp.bfloat16)
            send(near_sum.at[at, 0], last_in.at[at, 0], step_send_sem.at[1], last_sem.at[at], x_up, shard)
            near_sum[at, 1] = (
                near_in[at, 1].astype(jnp.float32) + part[at, down_x].astype(jnp.float32)
            ).astype(jnp.bfloat16)
            send(near_sum.at[at, 1], last_in.at[at, 1], step_send_sem.at[1], last_sem.at[at], x_down, shard)

        @pl.when(step < total)
        def _():
            send(part.at[step, up_x], last_in.at[step, 2], step_send_sem.at[2], last_sem.at[step], x_up, shard)
            send(part.at[step, 4 + down_x], last_in.at[step, 3], step_send_sem.at[2], last_sem.at[step], x_down, shard)

        @pl.when(step == 2)
        def _():
            wait(sq_all.at[pl.ds(0, 7)], sq_sem.at[1])
            squares_sum = sq_all[0]
            for idx in range(1, 8):
                squares_sum = squares_sum + sq_all[idx]
            row_scale[...] = lax.rsqrt(squares_sum / D + epsilon)

        @pl.when((step >= 2) & (step <= total + 1))
        def _():
            at = step - 2
            wait(last_in.at[at], last_sem.at[at])
            other = 1 - y_hi

            def group_sum(side):
                return (
                    part[at, 4 * side + x_pos].astype(jnp.float32)
                    + last_in[at, 1 - side].astype(jnp.float32)
                    + last_in[at, 2 + side].astype(jnp.float32)
                )

            pair_out[at] = group_sum(other).astype(jnp.bfloat16)
            send(pair_out.at[at], pair_in.at[at], step_send_sem.at[3], pair_sem.at[at], y_pair, shard)
            own_sum[at] = group_sum(y_hi)

        @pl.when(step >= 3)
        def _():
            at = step - 3
            wait(pair_in.at[at], pair_sem.at[at])
            scale = row_scale[pl.ds(at, 1), :]
            summed = own_sum[at] + pair_in[at].astype(jnp.float32)
            done[at] = jnp.where(scale > 0.0, summed * scale, 0.0).astype(jnp.bfloat16)

        @pl.when(step == TILES + 2)
        def _():
            for hop in range(8):
                to = z_at(hop)
                first = jnp.minimum(lax.shift_right_logical(starts[to * 4] - shard + 31, 5), TILES - 1)
                second = jnp.minimum(first + 1, TILES - 1)
                if hop == 0:
                    route_in[z_pos, 0] = done[first]
                    route_in[z_pos, 1] = done[second]
                else:
                    route_out[hop - 1, 0] = done[first]
                    route_out[hop - 1, 1] = done[second]
                    send(route_out.at[hop - 1], route_in.at[z_pos], route_sem.at[0], route_sem.at[1], group, z_mate(hop))

        return carry

    lax.fori_loop(0, total + 3, step_body, 0)

    send(
        done.at[pl.ds(TILES, rounds)],
        final.at[pl.ds(12 + rounds, rounds)],
        text_sem.at[0],
        text_sem.at[1],
        group,
        core_mate,
    )
    for idx in range(rounds):
        final[12 + idx] = done[TILES + idx]

    wait(route_in.at[pl.ds(0, 7)], route_sem.at[1])
    quad_start = starts[z_pos * 4]

    def routed(to, idx):
        begin = starts[z_pos * 4 + to]
        slot = begin + ((rank - begin) & 3) + 4 * idx
        slot = jnp.minimum(slot, SLOTS - 1)
        source = slot & 31
        first = lax.shift_right_logical(quad_start - source + 31, 5)
        place = jnp.maximum(jnp.minimum(lax.shift_right_logical(slot, 5) - first, 1), 0)
        return route_in[lax.shift_right_logical(source, 2), place]

    for step in (2, 3, 1):
        to = lax.rem(rank + step, 4)
        for idx in range(3):
            quad_out[step - 1, idx] = routed(to, idx)
        send(quad_out.at[step - 1], final.at[pl.ds(rank * 3, 3)], quad_sem.at[0], quad_sem.at[1], group, quad_mate(step))
    for idx in range(3):
        final[rank * 3 + idx] = routed(rank, idx)

    wait(final.at[pl.ds(0, 9)], quad_sem.at[1])
    wait(final.at[pl.ds(0, rounds)], text_sem.at[1])

    for block in range(BLOCKS):
        order = lax.rem(block - my_offset + BLOCKS, BLOCKS)
        image = ((my_start + order) & 3) * 3 + lax.shift_right_logical(order, 2)
        number = order - my_count + core * spare_0
        second = number >= cut
        text = jnp.where(second, number - cut, number)
        text = text + jnp.where(second == (core == 1), 12, 12 + rounds)
        place = jnp.where(order < my_count, image, text)
        place = jnp.maximum(jnp.minimum(place, 11 + 2 * rounds), 0)
        out_ref[:, block * TILE_ROWS : (block + 1) * TILE_ROWS] = final[place]

    wait(w_buf.at[pl.ds(0, 31)], w_send_sem)
    wait(got_buf, give_sem.at[0])
    wait(sq_all.at[pl.ds(0, 7)], sq_sem.at[0])
    wait(near_in, step_send_sem.at[0])
    wait(near_sum, step_send_sem.at[1])
    wait(near_in, step_send_sem.at[2])
    wait(pair_in, step_send_sem.at[3])
    wait(route_in.at[pl.ds(0, 7)], route_sem.at[0])
    wait(quad_out, quad_sem.at[0])
    wait(final.at[pl.ds(0, rounds)], text_sem.at[0])


def fast(rounds, collective, text_embed, vis_rows, norm_gain, w_kv, block_counts, block_offset):
    total = TILES + rounds
    padded = -(-total // 8) * 8
    tile = (TILE_ROWS, FEAT)
    keys = (KEYS, TILE_ROWS)
    bf16, f32 = jnp.bfloat16, jnp.float32
    smem = pl.BlockSpec(memory_space=pltpu.SMEM)
    vmem = pl.BlockSpec(memory_space=pltpu.VMEM)
    hbm = pl.BlockSpec(memory_space=pl.ANY)
    dma = pltpu.SemaphoreType.DMA
    return pl.pallas_call(
        functools.partial(kernel, rounds),
        out_shape=jax.ShapeDtypeStruct((KEYS, BLOCKS * TILE_ROWS), bf16),
        in_specs=[smem, smem, hbm, hbm, vmem, vmem],
        out_specs=vmem,
        scratch_shapes=[
            pltpu.SMEM((33,), jnp.int32),
            pltpu.VMEM((total,) + tile, bf16),
            pltpu.VMEM((BLOCKS,) + tile, bf16),
            pltpu.VMEM((rounds,) + tile, bf16),
            pltpu.VMEM((rounds,) + tile, bf16),
            pltpu.VMEM((32, 32, FEAT), bf16),
            pltpu.VMEM((total, 8) + keys, bf16),
            pltpu.VMEM((total, 2) + keys, bf16),
            pltpu.VMEM((total, 4) + keys, bf16),
            pltpu.VMEM((total, 2) + keys, bf16),
            pltpu.VMEM((total,) + keys, bf16),
            pltpu.VMEM((total,) + keys, f32),
            pltpu.VMEM((total,) + keys, bf16),
            pltpu.VMEM((total,) + keys, bf16),
            pltpu.VMEM((padded, TILE_ROWS), f32),
            pltpu.VMEM((8, padded, TILE_ROWS), f32),
            pltpu.VMEM((padded, TILE_ROWS), f32),
            pltpu.VMEM((7, 2) + keys, bf16),
            pltpu.VMEM((8, 2) + keys, bf16),
            pltpu.VMEM((3, 3) + keys, bf16),
            pltpu.VMEM((12 + 2 * rounds,) + keys, bf16),
            dma((2,)),
            dma,
            dma((2, 4)),
            dma,
            dma,
            dma((2,)),
            dma((2,)),
            dma((total,)),
            dma((total,)),
            dma((total,)),
            dma((4,)),
            dma((2,)),
            dma((2,)),
            dma((2,)),
        ],
        compiler_params=pltpu.CompilerParams(
            collective_id=collective,
            has_side_effects=True,
            vmem_limit_bytes=60 * 1024 * 1024,
        ),
        cost_estimate=pl.CostEstimate(flops=2 * total * 256 * 1024 * 1024, bytes_accessed=13 << 20, transcendentals=0),
    )(
        block_counts,
        block_offset,
        text_embed.reshape((BLOCKS,) + tile),
        vis_rows.reshape((TILES,) + tile),
        norm_gain.reshape(1, FEAT),
        w_kv.T,
    )


def slow(text_embed, vis_rows, norm_gain, w_kv, block_counts, block_offset):
    shard_count = lax.axis_size("seq")
    shard_id = lax.axis_index("seq")
    rows_dev, feat_dev = text_embed.shape
    w_full = lax.all_gather(w_kv, "seq", axis=1, tiled=True)
    run_ends = jnp.cumsum(block_counts)
    run_starts = run_ends - block_counts
    slot_ids = shard_id + shard_count * jnp.arange(TILES, dtype=jnp.int32)
    owners = jnp.sum((run_ends[None, :] <= slot_ids[:, None]).astype(jnp.int32), axis=1)
    peer_ids = jnp.arange(shard_count, dtype=jnp.int32)
    send_select = (peer_ids[:, None] == owners[None, :]).astype(jnp.bfloat16)
    order_in = (peer_ids - run_starts[shard_id]) % shard_count
    present = order_in < block_counts[shard_id]
    slot_block = (order_in + block_offset[shard_id]) % BLOCKS
    block_ids = jnp.arange(BLOCKS, dtype=jnp.int32)
    place_select = ((block_ids[:, None] == slot_block[None, :]) & present[None, :]).astype(jnp.bfloat16)
    vision_rows = jnp.repeat(jnp.sum(place_select.astype(jnp.float32), axis=1) > 0.5, TILE_ROWS)
    tile_flat = vis_rows.reshape(TILES, TILE_ROWS * feat_dev)
    outgoing = jnp.dot(send_select, tile_flat, preferred_element_type=jnp.float32).astype(jnp.bfloat16)
    incoming = lax.all_to_all(
        outgoing.reshape(shard_count, TILE_ROWS, feat_dev), "seq", split_axis=0, concat_axis=0, tiled=True
    )
    placed = jnp.dot(
        place_select, incoming.reshape(shard_count, TILE_ROWS * feat_dev), preferred_element_type=jnp.float32
    )
    placed = placed.astype(jnp.bfloat16).reshape(rows_dev, feat_dev)
    merged = jnp.where(vision_rows[:, None], placed, text_embed).astype(jnp.float32)
    squares = lax.psum(jnp.sum(merged * merged, axis=1), "section")
    normed = (merged * lax.rsqrt(squares / D + epsilon)[:, None] * norm_gain.astype(jnp.float32)).astype(jnp.bfloat16)
    term = lax.dot_general(w_full, normed, (((0,), (1,)), ((), ())), preferred_element_type=jnp.float32)
    return lax.psum_scatter(term.astype(jnp.bfloat16), "section", scatter_dimension=0, tiled=True)


ROUNDS = (4, 6)


def local(*args):
    block_counts = args[4]
    spare = 2 * BLOCKS - jnp.sum(block_counts.reshape(16, 2), axis=1)
    needed = jnp.max((spare + 1) // 2)
    branch = sum((needed > rounds).astype(jnp.int32) for rounds in ROUNDS)
    branches = [functools.partial(fast, rounds, idx) for idx, rounds in enumerate(ROUNDS)]
    return lax.switch(branch, branches + [slow], *args)


def solution(mesh):
    return jax.shard_map(
        local,
        mesh=mesh,
        in_specs=(
            P("seq", "section"),
            P("seq", "section"),
            P("section"),
            P("section", "seq"),
            P(),
            P(),
        ),
        out_specs=P("section", "seq"),
        check_vma=False,
    )
```

time: 651 us -> 147 us (0.23)
  waiting for transfers between devices: 480 us -> 0 us
  Pallas kernels: 0 us -> 127 us
  local copies, waits for them, and re-layouts: 65.2 us -> 4.08 us
  matrix products: 36 us -> 0 us
  blocking collectives: 34.4 us -> 0 us
  starting transfers between devices: 11.6 us -> 0 us
  other arithmetic: 9.36 us -> 0.77 us
    all_to_all x1 -> x0, waiting for transfers between devices: 360 us -> none  [local(): lax.all_to_all(outgoing, 'seq', split_axis=0, concat_axis=0, tiled=True)]
    pallas_call x0 -> x1, Pallas kernels: none -> 127 us  [fast(): pl.pallas_call(functools.partial(kernel, rounds), out_shape=jax.ShapeDtyp...]
    reduce_scatter x1 -> x0, waiting for transfers between devices: 119 us -> none  [project(): lax.psum_scatter(make_term(normed, w_full).astype(jnp.bfloat16), 'section...]
    unnamed x9 -> x1, local copies, waits for them, and re-layouts: 46 us -> 2.06 us
    dot_general x3 -> x0, matrix products: 36 us -> none  [the longest x1 13.2 us: make_term(): lax.dot_general(w_full, normed, (((0,), (1,)), ((), ())), preferred_eleme...]
    psum x1 -> x0, blocking collectives: 34.4 us -> none  [local(): squares = lax.psum(row_squares_of(merged), 'section')]
    reshape x2, local copies, waits for them, and re-layouts: 16.5 us -> 2.01 us  [the longest x1 1.28 us: fast(): norm_gain.reshape(1, FEAT)]
    all_to_all x1 -> x0, starting transfers between devices: 11.3 us -> none  [local(): lax.all_to_all(outgoing, 'seq', split_axis=0, concat_axis=0, tiled=True)]
  transfers between devices with their start and end apart: 3 -> 0, of which waited for: 2 -> 0; matrix products, arithmetic and copies ran while one was open for 8% -> 0% of each run, Pallas kernels for 0% -> 0%
where the time goes in v1:
time: 147 us; the launch traced here: 146 us
  Pallas kernels  127 us (86%)
  between operations  14.7 us (10%)
  local copies, waits for them, and re-layouts  4.08 us (3%)
    pallas_call x1, Pallas kernels, fast(): pl.pallas_call(functools.partial(kernel, rounds), out_shape=jax.ShapeDtyp...  127 us

profile of v1, /device:TPU:1, one launch (start us, length us, event | category | flops | bytes accessed | tf_op | source)
XLA Modules:
  0.0 146.4 jit_solution(8438957247335875121)
XLA Ops:
  6.5 0.7 reshape.91
  7.3 0.1 reduce_sum.36
  7.4 0.7 fusion.16
  9.3 128.1 %conditional.1 = (bf16[128,3072]{1,0:T(8,128)(2,1)}) conditional(s32[]{:T(128)} %clamp.3, (bf16[3072,1024]{1,0:T(8,128)(2,1)}, bf16[2816,1024]{1,0:T(8,128)(2,1)}, bf16[1024]{0:T(1024)(128)(2,1)}, bf16[1024,32]{0,1:T(8,128)(2,1)}, s32[32]{0:T(128)}, /*index=5*/s32[32]{0:T(128)}) %tuple.14, (bf16[3072,1024]{1,0:T(8,128)(2,1)}, ...), branch_computations={%region_2.3_spmd, %region_3.4_spmd, %region_4.11_spmd} | conditional | flops 9126805504 | bytes 261140864 | solution.py:473
  9.4 1.3 reshape.80.gain_ref
  10.6 126.6 %branch_0_fun.1 = bf16[128,3072]{1,0:T(8,128)(2,1)} custom-call(s32[32]{0:T(128)} %get-tuple-element.44.counts, s32[32]{0:T(128)} %get-tuple-element.46.offsets, bf16[12,256,1024]{2,1,0:T(8,128)(2,1)} %bitcast.23, bf16[11,256,1024]{2,1,0:T(8,128)(2,1)} %bitcast.25, bf16[1,1024]{1,0:T(2,128)(2,1)} %reshape.80.gain_ref, bf16[32,1024]{1,0:T(8,128)(2,1)} %bitcast.27), custom_call_target="tpu_custom_call" | custom-call | flops 8053063680 | bytes 13631488 | tf_op jit(solution)/shard_map/cond/branch_0_fun/pallas_call | solution.py:373
  137.5 2.1 %copy.39 = bf16[128,3072]{1,0:T(8,128)(2,1)} copy(bf16[128,3072]{1,0:T(8,128)(2,1)} %get-tuple-element.84) | data formatting | bytes 1572864

commit v2 on v1

--- a/solution.py
+++ b/solution.py
@@ -16,6 +16,10 @@
 KEYS = 128
 MESH = pl.DeviceIdType.MESH
 epsilon = 1e-06
+X_LAGS = (2, 4, 6)
+Y_LAGS = (4, 6, 8)
+FIRST_LAST = min(X_LAGS[2], Y_LAGS[2])
+LAG = max(X_LAGS[2], Y_LAGS[2])
 
 
 def kernel(
@@ -40,6 +44,8 @@
     pair_out,
     own_sum,
     pair_in,
+    half_in,
+    half_sum,
     done,
     sq_own,
     sq_all,
@@ -49,8 +55,8 @@
     quad_out,
     final,
     local_sem,
-    w_quad_sem,
     w_ring_sem,
+    w_y_sem,
     w_mate_sem,
     w_send_sem,
     give_sem,
@@ -58,6 +64,7 @@
     near_sem,
     last_sem,
     pair_sem,
+    half_sem,
     step_send_sem,
     route_sem,
     quad_sem,
@@ -69,20 +76,21 @@
     x_pos, y_hi = lax.rem(group, 4), lax.div(group, 4)
     z_pos, rank = lax.div(shard, 4), lax.rem(shard, 4)
     core = lax.rem(shard, 2)
-    half = core
+    turn = 1 - 2 * core
+    y_mate_rank = lax.rem(rank + 2, 4)
     x_up = y_hi * 4 + lax.rem(x_pos + 1, 4)
     x_down = y_hi * 4 + lax.rem(x_pos + 3, 4)
     y_pair = (1 - y_hi) * 4 + x_pos
-    core_mate = z_pos * 4 + rank + 1 - 2 * core
+    core_mate = z_pos * 4 + rank + turn
 
     def quad_mate(step):
         return z_pos * 4 + lax.rem(rank + step, 4)
 
-    def z_mate(step):
-        return lax.rem(z_pos + step, 8) * 4 + rank
-
     def z_at(step):
         return lax.rem(z_pos + step + 8, 8)
+
+    def z_mate(step):
+        return z_at(step) * 4 + rank
 
     def send(src, dst, send_sem, recv_sem, to_group, to_shard):
         pltpu.make_async_remote_copy(
@@ -114,7 +122,8 @@
         greet(group, quad_mate(step))
 
     sq_own[...] = jnp.zeros_like(sq_own)
-    w_buf[shard] = (wt_ref[...].astype(jnp.float32) * gain_ref[...].astype(jnp.float32)).astype(jnp.bfloat16)
+    gain = gain_ref[...].astype(jnp.float32).reshape(1, FEAT)
+    w_buf[shard] = (wt_ref[...].astype(jnp.float32) * gain).astype(jnp.bfloat16)
 
     def scan(idx, running):
         starts[idx] = running
@@ -129,8 +138,33 @@
 
     pl.semaphore_wait(barrier, 17)
 
-    for step in range(1, 4):
-        send(w_buf.at[shard], w_buf.at[shard], w_send_sem, w_quad_sem, group, quad_mate(step))
+    def w_piece(step, stream):
+        return w_buf.at[z_at(step) * 4 + (rank, y_mate_rank)[stream]]
+
+    def w_share(step, stream):
+        piece = w_piece(step, stream)
+        send(piece, piece, w_send_sem, w_mate_sem, group, core_mate)
+
+    def w_pass(step, stream):
+        up, down = w_piece(1 - step, stream), w_piece(step - 1, stream)
+        if step == 4:
+            up, down = up.at[pl.ds(0, 16)], down.at[pl.ds(16, 16)]
+        send(up, up, w_send_sem, w_ring_sem.at[stream, 0, step - 1], group, z_mate(1))
+        send(down, down, w_send_sem, w_ring_sem.at[stream, 1, step - 1], group, z_mate(7))
+
+    def w_take(step, stream):
+        piece = w_buf.at[0] if step < 4 else w_buf.at[0, pl.ds(0, 16)]
+        wait(piece, w_ring_sem.at[stream, 0, step - 1])
+        wait(piece, w_ring_sem.at[stream, 1, step - 1])
+        if step < 4:
+            w_pass(step + 1, stream)
+            w_share(-step, stream)
+        w_share(step, stream)
+
+    own_piece = w_piece(0, 0)
+    send(own_piece, own_piece, w_send_sem, w_y_sem, group, quad_mate(2))
+    w_pass(1, 0)
+    w_share(0, 0)
 
     text_copy.wait()
 
@@ -142,29 +176,9 @@
     lax.fori_loop(0, rounds, give, 0)
     send(give_buf, got_buf, give_sem.at[0], give_sem.at[1], group, core_mate)
 
-    wait(w_buf.at[pl.ds(0, 3)], w_quad_sem)
-
-    def w_half(quad):
-        return w_buf.at[pl.ds(quad * 4 + half * 2, 2)]
-
-    def w_mate_send(quad):
-        send(w_half(quad), w_half(quad), w_send_sem, w_mate_sem, group, core_mate)
-
-    def ring_step(step):
-        up, down = z_at(1 - step), z_at(step - 1)
-        if step < 4:
-            send(w_half(up), w_half(up), w_send_sem, w_ring_sem.at[0, step - 1], group, z_mate(1))
-            send(w_half(down), w_half(down), w_send_sem, w_ring_sem.at[1, step - 1], group, z_mate(7))
-        else:
-            up_piece = w_buf.at[up * 4 + half * 2]
-            down_piece = w_buf.at[down * 4 + half * 2 + 1]
-            send(up_piece, up_piece, w_send_sem, w_ring_sem.at[0, 3], group, z_mate(1))
-            send(down_piece, down_piece, w_send_sem, w_ring_sem.at[1, 3], group, z_mate(7))
-
-    def ring_wait(step):
-        pieces = 2 if step < 4 else 1
-        wait(w_buf.at[pl.ds(0, pieces)], w_ring_sem.at[0, step - 1])
-        wait(w_buf.at[pl.ds(0, pieces)], w_ring_sem.at[1, step - 1])
+    wait(w_buf.at[0], w_y_sem)
+    w_pass(1, 1)
+    w_share(0, 1)
 
     def squares(idx, carry):
         rows = x_buf[idx].astype(jnp.float32)
@@ -175,24 +189,18 @@
         sq_own[pl.ds(idx, 1), :] = jnp.sum(lanes.T, axis=0, keepdims=True)
         return carry
 
-    ring_step(1)
+    w_take(1, 0)
     vis_copy.wait()
-    lax.fori_loop(0, 4, squares, 0)
-    ring_wait(1)
-    ring_step(2)
-    w_mate_send(z_at(-1))
-    w_mate_send(z_at(1))
-    lax.fori_loop(4, 8, squares, 0)
-    ring_wait(2)
-    ring_step(3)
-    w_mate_send(z_at(-2))
-    w_mate_send(z_at(2))
-    lax.fori_loop(8, TILES, squares, 0)
-    ring_wait(3)
-    ring_step(4)
-    w_mate_send(z_at(-3))
-    w_mate_send(z_at(3))
-
+    lax.fori_loop(0, 2, squares, 0)
+    w_take(1, 1)
+    lax.fori_loop(2, 5, squares, 0)
+    w_take(2, 0)
+    lax.fori_loop(5, 7, squares, 0)
+    w_take(2, 1)
+    lax.fori_loop(7, 10, squares, 0)
+    w_take(3, 0)
+    lax.fori_loop(10, TILES, squares, 0)
+    w_take(3, 1)
     wait(got_buf, give_sem.at[1])
 
     def pick(idx, carry):
@@ -212,47 +220,91 @@
         send(sq_own, sq_all.at[group], sq_sem.at[0], sq_sem.at[1], lax.rem(group + step, 8), shard)
     sq_all[group] = sq_own[...]
 
-    ring_wait(4)
-    w_mate_send(z_at(4))
-    wait(w_buf.at[pl.ds(0, 14)], w_mate_sem)
+    w_take(4, 0)
+    w_take(4, 1)
+    wait(w_buf.at[pl.ds(0, 16)], w_mate_sem)
 
     far = lax.rem(x_pos + 2, 4)
     up_x = lax.rem(x_pos + 1, 4)
     down_x = lax.rem(x_pos + 3, 4)
+    low, high = pl.ds(0, KEYS // 2), pl.ds(KEYS // 2, KEYS // 2)
+
+    def first_tile(quad):
+        least = jnp.maximum(48 * quad - 32, 4 * quad)
+        return lax.shift_right_logical(jnp.maximum(least - shard + 31, 0), 5)
+
+    def last_tile(quad):
+        most = jnp.minimum(48 * quad + 47, 323 + 4 * quad)
+        return jnp.minimum(lax.shift_right_logical(jnp.maximum(most - shard, 0), 5), TILES - 1)
+
+    next_quad = z_at(turn)
+    base = jnp.minimum(jnp.where(core == 0, first_tile(next_quad), last_tile(next_quad)), TILES - 1)
+
+    def place_of(tile):
+        return lax.rem(turn * (tile - base) + TILES, TILES)
+
+    def tile_at(place):
+        return jnp.where(place < TILES, lax.rem(base + turn * place + TILES, TILES), place)
+
+    def ready_at(quad):
+        begin, end = first_tile(quad), last_tile(quad)
+        ready = jnp.int32(0)
+        for idx in range(4):
+            tile = jnp.minimum(jnp.minimum(begin + idx, end), TILES - 1)
+            ready = jnp.maximum(ready, place_of(tile))
+        return ready
+
+    ready = [ready_at(z_at(turn * hop)) for hop in range(8)]
+
+    def routed_from(quad, idx):
+        tile = lax.shift_right_logical(starts[quad * 4] - shard + 31, 5) + idx
+        return done[place_of(jnp.minimum(tile, TILES - 1))]
+
+    def finish(at, summed):
+        scale = row_scale[pl.ds(tile_at(at), 1), :]
+        done[at] = jnp.where(scale > 0.0, summed * scale, 0.0).astype(jnp.bfloat16)
+
+    def f32(value):
+        return value.astype(jnp.float32)
 
     def step_body(step, carry):
+        def on(lag, kind):
+            at = step - lag
+            return at, pl.when((at >= 0) & (at < total) & ((at & 1) == kind))
+
         @pl.when(step < total)
         def _():
-            rows = x_buf[step]
             res = lax.dot_general(
                 w_buf[...].reshape(1024, FEAT),
-                rows,
+                x_buf[tile_at(step)],
                 (((1,), (1,)), ((), ())),
                 preferred_element_type=jnp.float32,
             )
             part[step] = res.astype(jnp.bfloat16).reshape(8, KEYS, TILE_ROWS)
+
+        at, when = on(0, 0)
+
+        @when
+        def _():
             send(part.at[step, 4 + far], near_in.at[step, 0], step_send_sem.at[0], near_sem.at[step], x_up, shard)
             send(part.at[step, far], near_in.at[step, 1], step_send_sem.at[0], near_sem.at[step], x_down, shard)
-
-        @pl.when((step >= 1) & (step <= total))
-        def _():
-            at = step - 1
-            wait(near_in.at[at], near_sem.at[at])
-            near_sum[at, 0] = (
-                near_in[at, 0].astype(jnp.float32) + part[at, 4 + up_x].astype(jnp.float32)
-            ).astype(jnp.bfloat16)
-            send(near_sum.at[at, 0], last_in.at[at, 0], step_send_sem.at[1], last_sem.at[at], x_up, shard)
-            near_sum[at, 1] = (
-                near_in[at, 1].astype(jnp.float32) + part[at, down_x].astype(jnp.float32)
-            ).astype(jnp.bfloat16)
-            send(near_sum.at[at, 1], last_in.at[at, 1], step_send_sem.at[1], last_sem.at[at], x_down, shard)
-
-        @pl.when(step < total)
-        def _():
             send(part.at[step, up_x], last_in.at[step, 2], step_send_sem.at[2], last_sem.at[step], x_up, shard)
             send(part.at[step, 4 + down_x], last_in.at[step, 3], step_send_sem.at[2], last_sem.at[step], x_down, shard)
 
-        @pl.when(step == 2)
+        at, when = on(0, 1)
+
+        @when
+        def _():
+            send(
+                part.at[step, pl.ds(4 * (1 - y_hi), 4)],
+                half_in.at[lax.div(step, 2)],
+                step_send_sem.at[4],
+                half_sem.at[lax.div(step, 2)],
+                y_pair,
+                shard,
+            )
+
+        @pl.when(step == FIRST_LAST)
         def _():
             wait(sq_all.at[pl.ds(0, 7)], sq_sem.at[1])
             squares_sum = sq_all[0]
@@ -260,48 +312,84 @@
                 squares_sum = squares_sum + sq_all[idx]
             row_scale[...] = lax.rsqrt(squares_sum / D + epsilon)
 
-        @pl.when((step >= 2) & (step <= total + 1))
-        def _():
-            at = step - 2
+        at_pair, when = on(X_LAGS[2], 0)
+
+        @when
+        def _():
+            wait(pair_in.at[at_pair], pair_sem.at[at_pair])
+            finish(at_pair, own_sum[lax.div(at_pair, 2)] + f32(pair_in[at_pair]))
+
+        at_end, when = on(Y_LAGS[2], 1)
+
+        @when
+        def _():
+            at, half = at_end, lax.div(at_end, 2)
+            wait(last_in.at[at, pl.ds(0, 2)], last_sem.at[at])
+            low_sum = f32(half_sum[half, x_pos, low]) + f32(last_in[at, 0, high]) + f32(last_in[at, 1, low])
+            high_sum = f32(half_sum[half, x_pos, high]) + f32(last_in[at, 0, low]) + f32(last_in[at, 1, high])
+            finish(at, jnp.concatenate([low_sum, high_sum], axis=0))
+
+        at_last, when = on(X_LAGS[1], 0)
+
+        @when
+        def _():
+            at = at_last
             wait(last_in.at[at], last_sem.at[at])
             other = 1 - y_hi
 
             def group_sum(side):
-                return (
-                    part[at, 4 * side + x_pos].astype(jnp.float32)
-                    + last_in[at, 1 - side].astype(jnp.float32)
-                    + last_in[at, 2 + side].astype(jnp.float32)
-                )
+                return f32(part[at, 4 * side + x_pos]) + f32(last_in[at, 1 - side]) + f32(last_in[at, 2 + side])
 
             pair_out[at] = group_sum(other).astype(jnp.bfloat16)
             send(pair_out.at[at], pair_in.at[at], step_send_sem.at[3], pair_sem.at[at], y_pair, shard)
-            own_sum[at] = group_sum(y_hi)
-
-        @pl.when(step >= 3)
-        def _():
-            at = step - 3
-            wait(pair_in.at[at], pair_sem.at[at])
-            scale = row_scale[pl.ds(at, 1), :]
-            summed = own_sum[at] + pair_in[at].astype(jnp.float32)
-            done[at] = jnp.where(scale > 0.0, summed * scale, 0.0).astype(jnp.bfloat16)
-
-        @pl.when(step == TILES + 2)
-        def _():
-            for hop in range(8):
-                to = z_at(hop)
-                first = jnp.minimum(lax.shift_right_logical(starts[to * 4] - shard + 31, 5), TILES - 1)
-                second = jnp.minimum(first + 1, TILES - 1)
-                if hop == 0:
-                    route_in[z_pos, 0] = done[first]
-                    route_in[z_pos, 1] = done[second]
-                else:
-                    route_out[hop - 1, 0] = done[first]
-                    route_out[hop - 1, 1] = done[second]
-                    send(route_out.at[hop - 1], route_in.at[z_pos], route_sem.at[0], route_sem.at[1], group, z_mate(hop))
+            own_sum[lax.div(at, 2)] = group_sum(y_hi)
+
+        at_near, when = on(X_LAGS[0], 0)
+
+        @when
+        def _():
+            at = at_near
+            wait(near_in.at[at], near_sem.at[at])
+            near_sum[at, 0] = (f32(near_in[at, 0]) + f32(part[at, 4 + up_x])).astype(jnp.bfloat16)
+            send(near_sum.at[at, 0], last_in.at[at, 0], step_send_sem.at[1], last_sem.at[at], x_up, shard)
+            near_sum[at, 1] = (f32(near_in[at, 1]) + f32(part[at, down_x])).astype(jnp.bfloat16)
+            send(near_sum.at[at, 1], last_in.at[at, 1], step_send_sem.at[1], last_sem.at[at], x_down, shard)
+
+        at_hop, when = on(Y_LAGS[1], 1)
+
+        @when
+        def _():
+            at, half = at_hop, lax.div(at_hop, 2)
+            wait(near_in.at[at, 0], near_sem.at[at])
+            near_sum[at, 0, high] = (f32(near_in[at, 0, high]) + f32(half_sum[half, up_x, high])).astype(jnp.bfloat16)
+            near_sum[at, 1, low] = (f32(near_in[at, 0, low]) + f32(half_sum[half, down_x, low])).astype(jnp.bfloat16)
+            send(near_sum.at[at, 0, high], last_in.at[at, 0, low], step_send_sem.at[6], last_sem.at[at], x_up, shard)
+            send(near_sum.at[at, 1, low], last_in.at[at, 1, low], step_send_sem.at[6], last_sem.at[at], x_down, shard)
+
+        at_half, when = on(Y_LAGS[0], 1)
+
+        @when
+        def _():
+            at, half = at_half, lax.div(at_half, 2)
+            wait(half_in.at[half], half_sem.at[half])
+            half_sum[half] = (f32(part[at, pl.ds(4 * y_hi, 4)]) + f32(half_in[half])).astype(jnp.bfloat16)
+            send(half_sum.at[half, far, high], near_in.at[at, 0, high], step_send_sem.at[5], near_sem.at[at], x_up, shard)
+            send(half_sum.at[half, far, low], near_in.at[at, 0, low], step_send_sem.at[5], near_sem.at[at], x_down, shard)
+            send(half_sum.at[half, up_x, low], last_in.at[at, 0, high], step_send_sem.at[5], last_sem.at[at], x_up, shard)
+            send(half_sum.at[half, down_x, high], last_in.at[at, 1, high], step_send_sem.at[5], last_sem.at[at], x_down, shard)
+
+        for hop in range(1, 8):
+            to = z_at(turn * hop)
+
+            @pl.when(step == ready[hop] + LAG)
+            def _():
+                route_out[hop - 1, 0] = routed_from(to, 0)
+                route_out[hop - 1, 1] = routed_from(to, 1)
+                send(route_out.at[hop - 1], route_in.at[z_pos], route_sem.at[0], route_sem.at[1], group, to * 4 + rank)
 
         return carry
 
-    lax.fori_loop(0, total + 3, step_body, 0)
+    lax.fori_loop(0, total + LAG, step_body, 0)
 
     send(
         done.at[pl.ds(TILES, rounds)],
@@ -311,8 +399,8 @@
         group,
         core_mate,
     )
-    for idx in range(rounds):
-        final[12 + idx] = done[TILES + idx]
+    for idx in range(2):
+        route_in[z_pos, idx] = routed_from(z_pos, idx)
 
     wait(route_in.at[pl.ds(0, 7)], route_sem.at[1])
     quad_start = starts[z_pos * 4]
@@ -333,6 +421,8 @@
         send(quad_out.at[step - 1], final.at[pl.ds(rank * 3, 3)], quad_sem.at[0], quad_sem.at[1], group, quad_mate(step))
     for idx in range(3):
         final[rank * 3 + idx] = routed(rank, idx)
+    for idx in range(rounds):
+        final[12 + idx] = done[TILES + idx]
 
     wait(final.at[pl.ds(0, 9)], quad_sem.at[1])
     wait(final.at[pl.ds(0, rounds)], text_sem.at[1])
@@ -348,13 +438,16 @@
         place = jnp.maximum(jnp.minimum(place, 11 + 2 * rounds), 0)
         out_ref[:, block * TILE_ROWS : (block + 1) * TILE_ROWS] = final[place]
 
+    evens, odds = (total + 1) // 2, total // 2
     wait(w_buf.at[pl.ds(0, 31)], w_send_sem)
     wait(got_buf, give_sem.at[0])
     wait(sq_all.at[pl.ds(0, 7)], sq_sem.at[0])
-    wait(near_in, step_send_sem.at[0])
-    wait(near_sum, step_send_sem.at[1])
-    wait(near_in, step_send_sem.at[2])
-    wait(pair_in, step_send_sem.at[3])
+    for idx in range(3):
+        wait(near_in.at[pl.ds(0, evens)], step_send_sem.at[idx])
+    wait(pair_in.at[pl.ds(0, evens)], step_send_sem.at[3])
+    wait(half_in, step_send_sem.at[4])
+    wait(near_in.at[pl.ds(0, odds)], step_send_sem.at[5])
+    wait(pair_in.at[pl.ds(0, odds)], step_send_sem.at[6])
     wait(route_in.at[pl.ds(0, 7)], route_sem.at[0])
     wait(quad_out, quad_sem.at[0])
     wait(final.at[pl.ds(0, rounds)], text_sem.at[0])
@@ -387,8 +480,10 @@
             pltpu.VMEM((total, 4) + keys, bf16),
             pltpu.VMEM((total, 2) + keys, bf16),
             pltpu.VMEM((total,) + keys, bf16),
-            pltpu.VMEM((total,) + keys, f32),
+            pltpu.VMEM(((total + 1) // 2,) + keys, f32),
             pltpu.VMEM((total,) + keys, bf16),
+            pltpu.VMEM((total // 2, 4) + keys, bf16),
+            pltpu.VMEM((total // 2, 4) + keys, bf16),
             pltpu.VMEM((total,) + keys, bf16),
             pltpu.VMEM((padded, TILE_ROWS), f32),
             pltpu.VMEM((8, padded, TILE_ROWS), f32),
@@ -398,8 +493,8 @@
             pltpu.VMEM((3, 3) + keys, bf16),
             pltpu.VMEM((12 + 2 * rounds,) + keys, bf16),
             dma((2,)),
+            dma((2, 2, 4)),
             dma,
-            dma((2, 4)),
             dma,
             dma,
             dma((2,)),
@@ -407,7 +502,8 @@
             dma((total,)),
             dma((total,)),
             dma((total,)),
-            dma((4,)),
+            dma((total // 2,)),
+            dma((7,)),
             dma((2,)),
             dma((2,)),
             dma((2,)),
@@ -423,7 +519,7 @@
         block_offset,
         text_embed.reshape((BLOCKS,) + tile),
         vis_rows.reshape((TILES,) + tile),
-        norm_gain.reshape(1, FEAT),
+        norm_gain,
         w_kv.T,
     )
 

time: 147 us -> 122 us (0.83)
  Pallas kernels: 127 us -> 103 us
    pallas_call x1, Pallas kernels: 127 us -> 103 us  [fast(): pl.pallas_call(functools.partial(kernel, rounds), out_shape=jax.ShapeDtyp...]
where the time goes in v2:
time: 122 us
  Pallas kernels  103 us (84%)
  between operations  14.7 us (12%)
  local copies, waits for them, and re-layouts  2.8 us (2%)
    pallas_call x1, Pallas kernels, fast(): pl.pallas_call(functools.partial(kernel, rounds), out_shape=jax.ShapeDtyp...  103 us

profile of v2, /device:TPU:1, one launch (start us, length us, event | category | flops | bytes accessed | tf_op | source)
XLA Modules:
  0.0 121.7 jit_solution(1127691174276844880)
XLA Ops:
  6.5 0.7 reshape.85
  7.3 0.1 reduce_sum.36
  7.4 0.7 fusion.16
  9.3 103.5 %conditional.1 = (bf16[128,3072]{1,0:T(8,128)(2,1)}) conditional(s32[]{:T(128)} %clamp.3, (bf16[3072,1024]{1,0:T(8,128)(2,1)}, bf16[2816,1024]{1,0:T(8,128)(2,1)}, bf16[1024,32]{0,1:T(8,128)(2,1)}, s32[32]{0:T(128)}, s32[32]{0:T(128)}, /*index=5*/bf16[1024]{0:T(1024)(128)(2,1)}) %tuple.14, (bf16[3072,1024]{1,0:T(8,128)(2,1)}, ...), branch_computations={%region_2.3_spmd, %region_3.4_spmd, %region_4.11_spmd} | conditional | flops 9126805504 | bytes 261140864 | solution.py:569
  9.4 103.2 %branch_0_fun.1 = bf16[128,3072]{1,0:T(8,128)(2,1)} custom-call(s32[32]{0:T(128)} %get-tuple-element.44.counts, s32[32]{0:T(128)} %get-tuple-element.46.offsets, bf16[12,256,1024]{2,1,0:T(8,128)(2,1)} %bitcast.23, bf16[11,256,1024]{2,1,0:T(8,128)(2,1)} %bitcast.25, bf16[1024]{0:T(1024)(128)(2,1)} %get-tuple-element.49.gain_ref, bf16[32,1024]{1,0:T(8,128)(2,1)} %bitcast.27), custom_call_target="tpu_custom_call" | custom-call | flops 8053063680 | bytes 13631488 | tf_op jit(solution)/shard_map/cond/branch_0_fun/pallas_call | solution.py:466
  112.8 2.1 %copy.39 = bf16[128,3072]{1,0:T(8,128)(2,1)} copy(bf16[128,3072]{1,0:T(8,128)(2,1)} %get-tuple-element.84) | data formatting | bytes 1572864

commit v3 on v2

--- a/solution.py
+++ b/solution.py
@@ -17,7 +17,7 @@
 MESH = pl.DeviceIdType.MESH
 epsilon = 1e-06
 X_LAGS = (2, 4, 6)
-Y_LAGS = (4, 6, 8)
+Y_LAGS = (3, 5, 7)
 FIRST_LAST = min(X_LAGS[2], Y_LAGS[2])
 LAG = max(X_LAGS[2], Y_LAGS[2])
 
@@ -130,7 +130,8 @@
         return running + counts[idx]
 
     starts[32] = lax.fori_loop(0, 32, scan, jnp.int32(0))
-    my_count, my_offset, my_start = counts[shard], offsets[shard], starts[shard]
+    my_count, my_start = counts[shard], starts[shard]
+    my_offset, skipped = offsets[shard] & 15, lax.shift_right_logical(offsets[shard], 4)
     spare_0 = BLOCKS - counts[shard - core]
     spare_1 = BLOCKS - counts[shard - core + 1]
     spare = spare_0 + spare_1
@@ -204,7 +205,7 @@
     wait(got_buf, give_sem.at[1])
 
     def pick(idx, carry):
-        number = jnp.maximum(jnp.minimum(idx + core * cut, spare - 1), 0)
+        number = jnp.maximum(jnp.minimum(idx + skipped + core * cut, spare - 1), 0)
         of_first = number < spare_0
         mine = of_first == (core == 0)
         order = jnp.where(of_first, number, number - spare_0)
@@ -264,13 +265,53 @@
         scale = row_scale[pl.ds(tile_at(at), 1), :]
         done[at] = jnp.where(scale > 0.0, summed * scale, 0.0).astype(jnp.bfloat16)
 
+        @pl.when(at >= TILES)
+        def _():
+            final[12 + at - TILES] = done[at]
+            send(
+                done.at[at], final.at[12 + rounds + at - TILES], text_sem.at[0], text_sem.at[1], group, core_mate
+            )
+
     def f32(value):
         return value.astype(jnp.float32)
+
+    quad_start = starts[z_pos * 4]
+
+    def routed(to, idx):
+        begin = starts[z_pos * 4 + to]
+        slot = begin + ((rank - begin) & 3) + 4 * idx
+        slot = jnp.minimum(slot, SLOTS - 1)
+        source = slot & 31
+        first = lax.shift_right_logical(quad_start - source + 31, 5)
+        place = jnp.maximum(jnp.minimum(lax.shift_right_logical(slot, 5) - first, 1), 0)
+        return route_in[lax.shift_right_logical(source, 2), place]
+
+    def quad_exchange():
+        for idx in range(2):
+            route_in[z_pos, idx] = routed_from(z_pos, idx)
+        wait(route_in.at[pl.ds(0, 7)], route_sem.at[1])
+        for step in (2, 3, 1):
+            to = lax.rem(rank + step, 4)
+            for idx in range(3):
+                quad_out[step - 1, idx] = routed(to, idx)
+            send(
+                quad_out.at[step - 1],
+                final.at[pl.ds(rank * 3, 3)],
+                quad_sem.at[0],
+                quad_sem.at[1],
+                group,
+                quad_mate(step),
+            )
+        for idx in range(3):
+            final[rank * 3 + idx] = routed(rank, idx)
+
+    steps = max(total - 2 + Y_LAGS[2], total + X_LAGS[2])
 
     def step_body(step, carry):
         def on(lag, kind):
             at = step - lag
-            return at, pl.when((at >= 0) & (at < total) & ((at & 1) == kind))
+            y_first = ((at & 1) == 0) & (at < total - 1)
+            return at, pl.when((at >= 0) & (at < total) & (y_first == (kind == 1)))
 
         @pl.when(step < total)
         def _():
@@ -304,6 +345,10 @@
                 shard,
             )
 
+        @pl.when(step == steps - 1)
+        def _():
+            quad_exchange()
+
         @pl.when(step == FIRST_LAST)
         def _():
             wait(sq_all.at[pl.ds(0, 7)], sq_sem.at[1])
@@ -389,40 +434,7 @@
 
         return carry
 
-    lax.fori_loop(0, total + LAG, step_body, 0)
-
-    send(
-        done.at[pl.ds(TILES, rounds)],
-        final.at[pl.ds(12 + rounds, rounds)],
-        text_sem.at[0],
-        text_sem.at[1],
-        group,
-        core_mate,
-    )
-    for idx in range(2):
-        route_in[z_pos, idx] = routed_from(z_pos, idx)
-
-    wait(route_in.at[pl.ds(0, 7)], route_sem.at[1])
-    quad_start = starts[z_pos * 4]
-
-    def routed(to, idx):
-        begin = starts[z_pos * 4 + to]
-        slot = begin + ((rank - begin) & 3) + 4 * idx
-        slot = jnp.minimum(slot, SLOTS - 1)
-        source = slot & 31
-        first = lax.shift_right_logical(quad_start - source + 31, 5)
-        place = jnp.maximum(jnp.minimum(lax.shift_right_logical(slot, 5) - first, 1), 0)
-        return route_in[lax.shift_right_logical(source, 2), place]
-
-    for step in (2, 3, 1):
-        to = lax.rem(rank + step, 4)
-        for idx in range(3):
-            quad_out[step - 1, idx] = routed(to, idx)
-        send(quad_out.at[step - 1], final.at[pl.ds(rank * 3, 3)], quad_sem.at[0], quad_sem.at[1], group, quad_mate(step))
-    for idx in range(3):
-        final[rank * 3 + idx] = routed(rank, idx)
-    for idx in range(rounds):
-        final[12 + idx] = done[TILES + idx]
+    lax.fori_loop(0, steps, step_body, 0)
 
     wait(final.at[pl.ds(0, 9)], quad_sem.at[1])
     wait(final.at[pl.ds(0, rounds)], text_sem.at[1])
@@ -432,7 +444,7 @@
         image = ((my_start + order) & 3) * 3 + lax.shift_right_logical(order, 2)
         number = order - my_count + core * spare_0
         second = number >= cut
-        text = jnp.where(second, number - cut, number)
+        text = jnp.where(second, number - cut, number) - skipped
         text = text + jnp.where(second == (core == 1), 12, 12 + rounds)
         place = jnp.where(order < my_count, image, text)
         place = jnp.maximum(jnp.minimum(place, 11 + 2 * rounds), 0)
@@ -525,36 +537,21 @@
 
 
 def slow(text_embed, vis_rows, norm_gain, w_kv, block_counts, block_offset):
-    shard_count = lax.axis_size("seq")
-    shard_id = lax.axis_index("seq")
-    rows_dev, feat_dev = text_embed.shape
-    w_full = lax.all_gather(w_kv, "seq", axis=1, tiled=True)
-    run_ends = jnp.cumsum(block_counts)
-    run_starts = run_ends - block_counts
-    slot_ids = shard_id + shard_count * jnp.arange(TILES, dtype=jnp.int32)
-    owners = jnp.sum((run_ends[None, :] <= slot_ids[:, None]).astype(jnp.int32), axis=1)
-    peer_ids = jnp.arange(shard_count, dtype=jnp.int32)
-    send_select = (peer_ids[:, None] == owners[None, :]).astype(jnp.bfloat16)
-    order_in = (peer_ids - run_starts[shard_id]) % shard_count
-    present = order_in < block_counts[shard_id]
-    slot_block = (order_in + block_offset[shard_id]) % BLOCKS
-    block_ids = jnp.arange(BLOCKS, dtype=jnp.int32)
-    place_select = ((block_ids[:, None] == slot_block[None, :]) & present[None, :]).astype(jnp.bfloat16)
-    vision_rows = jnp.repeat(jnp.sum(place_select.astype(jnp.float32), axis=1) > 0.5, TILE_ROWS)
-    tile_flat = vis_rows.reshape(TILES, TILE_ROWS * feat_dev)
-    outgoing = jnp.dot(send_select, tile_flat, preferred_element_type=jnp.float32).astype(jnp.bfloat16)
-    incoming = lax.all_to_all(
-        outgoing.reshape(shard_count, TILE_ROWS, feat_dev), "seq", split_axis=0, concat_axis=0, tiled=True
-    )
-    placed = jnp.dot(
-        place_select, incoming.reshape(shard_count, TILE_ROWS * feat_dev), preferred_element_type=jnp.float32
-    )
-    placed = placed.astype(jnp.bfloat16).reshape(rows_dev, feat_dev)
-    merged = jnp.where(vision_rows[:, None], placed, text_embed).astype(jnp.float32)
-    squares = lax.psum(jnp.sum(merged * merged, axis=1), "section")
-    normed = (merged * lax.rsqrt(squares / D + epsilon)[:, None] * norm_gain.astype(jnp.float32)).astype(jnp.bfloat16)
-    term = lax.dot_general(w_full, normed, (((0,), (1,)), ((), ())), preferred_element_type=jnp.float32)
-    return lax.psum_scatter(term.astype(jnp.bfloat16), "section", scatter_dimension=0, tiled=True)
+    rounds, collective = ROUNDS[-1], len(ROUNDS) - 1
+    first, second = [
+        fast(rounds, collective, text_embed, vis_rows, norm_gain, w_kv, block_counts, block_offset + 16 * skipped)
+        for skipped in (0, rounds)
+    ]
+    shard = lax.axis_index("seq")
+    core = shard % 2
+    spare_0 = BLOCKS - block_counts[shard - core]
+    cut = (spare_0 + BLOCKS - block_counts[shard - core + 1] + 1) // 2
+    order = (jnp.arange(BLOCKS, dtype=jnp.int32) - block_offset[shard]) % BLOCKS
+    number = order - block_counts[shard]
+    place = number + core * spare_0
+    place = jnp.where(place >= cut, place - cut, place)
+    late = (number >= 0) & (place >= rounds)
+    return jnp.where(jnp.repeat(late, TILE_ROWS)[None, :], second, first)
 
 
 ROUNDS = (4, 6)
@@ -562,9 +559,9 @@
 
 def local(*args):
     block_counts = args[4]
-    spare = 2 * BLOCKS - jnp.sum(block_counts.reshape(16, 2), axis=1)
-    needed = jnp.max((spare + 1) // 2)
-    branch = sum((needed > rounds).astype(jnp.int32) for rounds in ROUNDS)
+    spare = 2 * BLOCKS - block_counts[:-1] - block_counts[1:]
+    spare = jnp.max(jnp.where(jnp.arange(31) % 2 == 0, spare, 0))
+    branch = sum((spare > 2 * rounds).astype(jnp.int32) for rounds in ROUNDS)
     branches = [functools.partial(fast, rounds, idx) for idx, rounds in enumerate(ROUNDS)]
     return lax.switch(branch, branches + [slow], *args)
 

time: 122 us -> 224 us (1.84)
  Pallas kernels: 103 us -> 211 us
  between operations: 14.7 us -> 1.31 us
  other arithmetic: 0.77 us -> 5.16 us
  loops' own time: 0.24 us -> 2.51 us
    pallas_call x1 -> x2, Pallas kernels: 103 us -> 211 us  [fast(): pl.pallas_call(functools.partial(kernel, rounds), out_shape=jax.ShapeDtyp...]
    dynamic_slice x0 -> x2, local copies, waits for them, and re-layouts: none -> 2.74 us  [the longest x1 1.42 us: slow(): number = order - block_counts[shard]]
    another operation x1, loops' own time: 0.24 us -> 2.51 us  [local(): return lax.switch(branch, branches + [slow], *args)]
where the time goes in v3:
time: 224 us
  Pallas kernels  211 us (94%)
  other arithmetic  5.16 us (2%)
  local copies, waits for them, and re-layouts  3.74 us (2%)
  loops' own time  2.51 us (1%)
    pallas_call x2, Pallas kernels, fast(): pl.pallas_call(functools.partial(kernel, rounds), out_shape=jax.ShapeDtyp...  211 us

profile of v3, /device:TPU:1, one launch (start us, length us, event | category | flops | bytes accessed | tf_op | source)
XLA Modules:
  0.0 223.6 jit_solution(6754394292061571686)
XLA Ops:
  0.0 1.4 fusion.1
  2.7 220.0 %conditional.1 = (bf16[128,3072]{1,0:T(8,128)(2,1)S(1)}) conditional(s32[]{:T(128)} %clamp.3, (bf16[3072,1024]{1,0:T(8,128)(2,1)}, bf16[2816,1024]{1,0:T(8,128)(2,1)}, bf16[1024,32]{0,1:T(8,128)(2,1)}, s32[32]{0:T(128)}, s32[32]{0:T(128)}, /*index=5*/bf16[1024]{0:T(1024)(128)(2,1)}) %tuple.14, (bf16[3072,1024]{1,0:T(8,128)(2,1)}, ...), branch_computations={%region_1.2_spmd, %region_2.3_spmd, %region_3.4_spmd} | conditional | flops 18254004224 | bytes 33052580 | solution.py:566
  3.0 1.3 dynamic_slice.8
  4.3 1.4 fusion.2
  7.7 1.3 compare_and_fusion
  8.9 1.2 broadcast_add_fusion.offsets
  10.2 0.1 broadcast_in_dim.12
  10.3 0.0 copy-start.1
  10.3 0.0 copy-start.2
  10.3 0.0 copy-start.3
  10.3 0.0 copy-start.4
  10.3 109.2 %branch_2_fun.2 = bf16[128,3072]{1,0:T(8,128)(2,1)} custom-call(s32[32]{0:T(128)} %get-tuple-element.58.counts, s32[32]{0:T(128)} %broadcast_add_fusion.offsets, bf16[12,256,1024]{2,1,0:T(8,128)(2,1)} %bitcast.15, bf16[11,256,1024]{2,1,0:T(8,128)(2,1)} %bitcast.19, bf16[1024]{0:T(1024)(128)(2,1)} %get-tuple-element.61.gain_ref, bf16[32,1024]{1,0:T(8,128)(2,1)} %bitcast.23), custom_call_target="tpu_custom_call" | custom-call | flops 9126805504 | bytes 13631488 | tf_op jit(solution)/shard_map/cond/branch_2_fun/pallas_call | solution.py:478
  119.6 0.0 copy-done.1
  119.6 0.0 copy-done.2
  119.6 0.0 copy-done.3
  119.6 0.0 copy-done.4
  119.6 0.0 copy-start
  119.6 101.6 %branch_2_fun.3 = bf16[128,3072]{1,0:T(8,128)(2,1)} custom-call(s32[32]{0:T(128)S(1)} %copy-done.1, s32[32]{0:T(128)S(1)} %copy-done.4, bf16[12,256,1024]{2,1,0:T(8,128)(2,1)} %bitcast.16, bf16[11,256,1024]{2,1,0:T(8,128)(2,1)} %bitcast.20, bf16[1024]{0:T(1024)(128)(2,1)S(1)} %copy-done.3, bf16[32,1024]{1,0:T(8,128)(2,1)S(1)} %bitcast.24), custom_call_target="tpu_custom_call" | custom-call | flops 9126805504 | bytes 13631488 | tf_op jit(solution)/shard_map/cond/branch_2_fun/pallas_call | solution.py:478
  221.2 0.0 copy-done
  221.3 1.2 broadcast_select_fusion
  222.7 0.9 copy.14
  (1 shorter events, 0.0 us)
Async XLA Ops:
  10.3 109.3 %copy-start.1 = (s32[32]{0:T(128)S(1)}, s32[32]{0:T(128)}, u32[]{:S(2)}) copy-start(s32[32]{0:T(128)} %get-tuple-element.58.counts) | copy-start | bytes 388 | tf_op jit(solution)/shard_map/cond
  10.3 109.3 %copy-start.2 = (bf16[1024,32]{0,1:T(8,128)(2,1)S(1)}, bf16[1024,32]{0,1:T(8,128)(2,1)}, u32[]{:S(2)}) copy-start(bf16[1024,32]{0,1:T(8,128)(2,1)} %get-tuple-element.62) | copy-start | bytes 196612 | tf_op jit(solution)/shard_map/cond
  10.3 109.3 %copy-start.3 = (bf16[1024]{0:T(1024)(128)(2,1)S(1)}, bf16[1024]{0:T(1024)(128)(2,1)}, u32[]{:S(2)}) copy-start(bf16[1024]{0:T(1024)(128)(2,1)} %get-tuple-element.61.gain_ref) | copy-start | bytes 6148 | tf_op jit(solution)/shard_map/cond
  10.3 109.3 %copy-start.4 = (s32[32]{0:T(128)S(1)}, s32[32]{0:T(128)}, u32[]{:S(2)}) copy-start(s32[32]{0:T(128)} %get-tuple-element.57.offsets) | copy-start | bytes 388 | tf_op jit(solution)/shard_map/cond
  119.6 101.6 %copy-start = (bf16[128,3072]{1,0:T(8,128)(2,1)S(1)}, bf16[128,3072]{1,0:T(8,128)(2,1)}, u32[]{:S(2)}) copy-start(bf16[128,3072]{1,0:T(8,128)(2,1)} %branch_2_fun.2) | copy-start | bytes 2359300 | tf_op jit(solution)/shard_map/cond
